TPU v7x, 32 devices: a whole 2x2x4 slice. The times are simulated.
32 devices in a mesh: groups: 2 (over y), batch: 4 (over x, core), mp: 4 (over z).
Axes of the slice: x: 2, y: 2, z: 4, core: 2. Of those that a mesh axis runs over, the one named last changes fastest.
Arguments:
- tokens: bfloat16 [512, 8192], P(('groups', 'batch')), parts along dimension 0, may hold values from -6 to 6
- gate_weight: bfloat16 [8192, 26624], P('batch', 'mp'), may hold values from -0.0625 to 0.0625
- up_weight: bfloat16 [8192, 26624], P('batch', 'mp'), may hold values from -0.0625 to 0.0625
- down_weight: bfloat16 [26624, 8192], P('mp', 'batch'), may hold values from -0.0390625 to 0.0390625
Outputs:
- mixed: bfloat16 [512, 8192], P(('groups', 'mp'), 'batch'), parts along dimension 0
There are 2 independent parts, one for each index of `groups`. A program takes and returns all parts, laid end to end along the dimension named above; an argument that names none is the same for every part. Nothing has to cross between parts.
All inputs are finite; a program needn't handle non-finite values.
Results may differ from a plain program's by a relative error of at most 0.017.
Values may be sent and summed in bfloat16 or wider, within the bound.
A program may use at most 192 MiB of HBM per device.

v0:
```python
import jax
import jax.numpy as jnp
from jax import lax
from jax.sharding import PartitionSpec as P


def local(tokens, gate_weight, up_weight, down_weight):
    hidden_width = gate_weight.shape[1]
    exchanged = lax.all_to_all(tokens, "batch", split_axis=1, concat_axis=0, tiled=True)
    both_weights = jnp.concatenate([gate_weight, up_weight], axis=1)
    summed = lax.psum_scatter(
        jnp.dot(exchanged, both_weights, preferred_element_type=jnp.float32).astype(jnp.bfloat16),
        "batch",
        scatter_dimension=0,
        tiled=True,
    ).astype(jnp.float32)
    hidden = (jax.nn.silu(summed[:, :hidden_width]) * summed[:, hidden_width:]).astype(jnp.bfloat16)
    terms = jnp.dot(
        lax.all_gather(hidden, "batch", axis=0, tiled=True),
        down_weight,
        preferred_element_type=jnp.float32,
    )
    shared = lax.psum_scatter(
        terms.astype(jnp.bfloat16), "mp", scatter_dimension=0, tiled=True
    ).astype(jnp.float32)
    row_count = shared.shape[0]
    own_part = lax.dynamic_slice_in_dim(exchanged, lax.axis_index("mp") * row_count, row_count, 0)
    return (own_part.astype(jnp.float32) + shared).astype(jnp.bfloat16)


def solution(mesh):
    placed = (P(("groups", "batch"), None), P("batch", "mp"), P("batch", "mp"), P("mp", "batch"))
    return jax.shard_map(
        local, mesh=mesh, in_specs=placed, out_specs=P(("groups", "mp"), "batch"), check_vma=False
    )
```

profile of v0, /device:TPU:0, one launch (start us, length us, event | category | flops | bytes accessed | tf_op | source)
XLA Modules:
  0.0 210.6 jit_solution(6348296578900358484)
XLA Ops:
  6.5 0.0 reduce-scatter.7.cloned.1.call-start
  6.5 1.3 copy.14
  7.8 18.5 %all_to_all.19 = bf16[64,4,2048]{2,0,1:T(8,128)(2,1)S(1)} all-to-all(bf16[64,4,2048]{2,0,1:T(8,128)(2,1)S(1)} %bitcast.13), channel_id=1, replica_groups=mesh['groups'=2,'batch'=4,'mp'=4] {'batch'}, dimensions={1} | all-to-all | bytes 2097152 | tf_op jit(solution)/shard_map/all_to_all | solution.py:9
  26.3 28.8 %fusion.7 = bf16[256,13312]{0,1:T(8,128)(2,1)} fusion(bf16[256,2048]{1,0:T(8,128)(2,1)S(1)} %bitcast.14, bf16[2048,6656]{1,0:T(8,128)(2,1)} %param.6, bf16[2048,6656]{1,0:T(8,128)(2,1)} %param.5), kind=kOutput, calls=%fused_computation.5 | convolution fusion | flops 14071103488 | bytes 62390272 | tf_op jit(solution)/shard_map/dot_general | solution.py:12
  55.1 10.0 %copy.10 = bf16[256,13312]{1,0:T(8,128)(2,1)} copy(bf16[256,13312]{0,1:T(8,128)(2,1)} %fusion.7) | data formatting | bytes 13631488
  65.1 0.0 reduce-scatter.7.cloned.1.call-update
  65.1 0.0 all-gather.2.cloned.1.call-start
  65.2 62.3 %reduce-scatter.7.cloned.1.call-done = bf16[64,13312]{1,0:T(8,128)(2,1)} async-done(((bf16[256,13312]{1,0:T(8,128)(2,1)}), bf16[64,13312]{1,0:T(8,128)(2,1)}) %reduce-scatter.7.cloned.1.call-update) | async-done | bytes 1703952 | tf_op jit(solution)/shard_map/reduce_scatter | solution.py:11
  127.5 1.7 convert_element_type.27
  129.2 1.4 fusion.10
  130.6 0.0 all-gather.2.cloned.1.call-update
  130.6 0.0 reduce-scatter.5.cloned.1.call-start
  130.6 30.1 %all-gather.2.cloned.1.call-done = bf16[256,6656]{1,0:T(8,128)(2,1)} async-done(((bf16[64,6656]{1,0:T(8,128)(2,1)}), bf16[256,6656]{1,0:T(8,128)(2,1)}) %all-gather.2.cloned.1.call-update) | async-done | bytes 3407888 | tf_op jit(solution)/shard_map/all_gather | solution.py:19
  160.8 14.2 %convolution_convert_fusion = bf16[256,2048]{1,0:T(8,128)(2,1)} fusion(bf16[256,6656]{1,0:T(8,128)(2,1)} %all-gather.2.cloned.1.call-done, bf16[6656,2048]{1,0:T(8,128)(2,1)} %param.7), kind=kOutput, calls=%fused_computation.6 | convolution fusion | flops 6979846144 | bytes 31719424 | tf_op jit(solution)/shard_map/dot_general | solution.py:18
  175.0 0.0 reduce-scatter.5.cloned.1.call-update
  175.0 27.3 %reduce-scatter.5.cloned.1.call-done = bf16[64,2048]{1,0:T(8,128)(2,1)} async-done(((bf16[256,2048]{1,0:T(8,128)(2,1)}), bf16[64,2048]{1,0:T(8,128)(2,1)}) %reduce-scatter.5.cloned.1.call-update) | async-done | bytes 262160 | tf_op jit(solution)/shard_map/reduce_scatter | solution.py:23
  202.3 1.7 add_convert_fusion
Async XLA Ops:
  6.5 121.0 %reduce-scatter.7.cloned.1.call-start = ((), (), s32[]{:S(2)}) async-start(), calls=%async_computation.5 | async-start | bytes 8519680 | tf_op jit(solution)/shard_map/reduce_scatter | solution.py:11
  65.1 95.6 %all-gather.2.cloned.1.call-start = ((), (), s32[]{:S(2)}) async-start(), calls=%async_computation.3 | async-start | bytes 4259840 | tf_op jit(solution)/shard_map/all_gather | solution.py:19
  130.6 71.8 %reduce-scatter.5.cloned.1.call-start = ((), (), s32[]{:S(2)}) async-start(), calls=%async_computation.4 | async-start | bytes 1310720 | tf_op jit(solution)/shard_map/reduce_scatter | solution.py:23
Sparse Core Ops, SparseCore 0:
  65.2 62.2 reduce-scatter.6
  130.7 30.0 all-gather.1
  175.2 27.1 reduce-scatter.4
where the time goes:
time: 211 us
  waiting for transfers between devices  120 us (57%)
  matrix products  43.1 us (20%)
  blocking collectives  18.5 us (9%)
  between operations  13.1 us (6%)
  local copies, waits for them, and re-layouts  11.3 us (5%)
  other arithmetic  4.76 us (2%)
    reduce_scatter x1, waiting for transfers between devices, local(): lax.psum_scatter(jnp.dot(exchanged, both_weights, preferred_element_type=...  62.3 us
    all_gather x1, waiting for transfers between devices, local(): lax.all_gather(hidden, 'batch', axis=0, tiled=True)  30.1 us
    dot_general x1, matrix products, local(): jnp.dot(exchanged, both_weights, preferred_element_type=jnp.float32)  28.8 us
    reduce_scatter x1, waiting for transfers between devices, local(): lax.psum_scatter(terms.astype(jnp.bfloat16), 'mp', scatter_dimension=0, t...  27.3 us
    all_to_all x1, blocking collectives, local(): lax.all_to_all(tokens, 'batch', split_axis=1, concat_axis=0, tiled=True)  18.5 us
    dot_general x1, matrix products, local(): jnp.dot(lax.all_gather(hidden, 'batch', axis=0, tiled=True), down_weight,...  14.2 us
    unnamed x1, local copies, waits for them, and re-layouts  9.97 us
  transfers between devices with their start and end apart: 3, of which 3 were waited for; matrix products, arithmetic and copies ran while one was open for 0% of the time, Pallas kernels for 0%

commit v1 on v0

--- a/solution.py
+++ b/solution.py
@@ -1,10 +1,269 @@
+import functools
+
 import jax
 import jax.numpy as jnp
 from jax import lax
+from jax.experimental import pallas as pl
+from jax.experimental.pallas import tpu as pltpu
 from jax.sharding import PartitionSpec as P
 
-
-def local(tokens, gate_weight, up_weight, down_weight):
+MESH = pl.DeviceIdType.MESH
+SLOTS = 3
+LAG_C, LAG_D, LAG_E = 3, 4, 5
+
+
+def kernel(
+    mp, chunks, tokens, gate_w, up_w, down_w, out,
+    acts, gate_s, up_s, down_s, away, kept, from_core, from_x, hid, total, line_out, line_in,
+    own_sem, gate_sem, up_sem, down_sem, tok_send, tok_recv,
+    core_send, core_recv, x_send, x_recv, hx_send, hx_recv, hc_send, hc_recv, hf_send, hf_recv,
+    line_send, line_recv,
+):
+    f32, bf16 = jnp.float32, jnp.bfloat16
+    me, z = lax.axis_index("batch"), lax.axis_index("mp")
+    x, c = lax.div(me, 2), lax.rem(me, 2)
+    sibling, across, diagonal = x * 2 + 1 - c, (1 - x) * 2 + c, (1 - x) * 2 + 1 - c
+    rows, depth = tokens.shape[0], acts.shape[1]
+    width = hid.shape[2]
+    tile = min(256, width)
+
+    def block(r):
+        return pl.ds(r * rows, rows)
+
+    def weights(i, ref, slots, sem, axis):
+        window = pl.ds(pl.multiple_of(i * width, width), width)
+        src = ref.at[:, window] if axis else ref.at[window, :]
+        slot = lax.rem(i, SLOTS)
+        return pltpu.make_async_copy(src, slots.at[slot], sem.at[slot])
+
+    def gate_up(i):
+        return weights(i, gate_w, gate_s, gate_sem, 1), weights(i, up_w, up_s, up_sem, 1)
+
+    def down(i):
+        return weights(i, down_w, down_s, down_sem, 0)
+
+    def remote(src, dst, send, recv, **place):
+        return pltpu.make_async_remote_copy(
+            src_ref=src, dst_ref=dst, send_sem=send, recv_sem=recv, device_id=place, device_id_type=MESH
+        )
+
+    def columns(index):
+        return pl.ds(pl.multiple_of(index * depth, depth), depth)
+
+    own_copy = pltpu.make_async_copy(tokens.at[:, columns(me)], acts.at[block(0), :], own_sem)
+    own_copy.start()
+    for i in range(SLOTS):
+        for copy in gate_up(i):
+            copy.start()
+    for i in range(SLOTS):
+        down(i).start()
+
+    barrier = pltpu.get_barrier_semaphore()
+    for peer in (sibling, across, diagonal):
+        pl.semaphore_signal(barrier, inc=1, device_id={"batch": peer}, device_id_type=MESH)
+
+    @pl.when(z > 0)
+    def _():
+        pl.semaphore_signal(barrier, inc=1, device_id={"mp": z - 1}, device_id_type=MESH)
+
+    @pl.when(z < mp - 1)
+    def _():
+        pl.semaphore_signal(barrier, inc=1, device_id={"mp": z + 1}, device_id_type=MESH)
+
+    @pl.when((z > 0) & (z < mp - 1))
+    def _():
+        pl.semaphore_wait(barrier, 5)
+
+    @pl.when((z == 0) | (z == mp - 1))
+    def _():
+        pl.semaphore_wait(barrier, 4)
+
+    token_copies = [
+        remote(tokens.at[:, columns(peer)], acts.at[block(r), :], tok_send.at[r], tok_recv.at[r], batch=peer)
+        for r, peer in ((1, across), (3, diagonal), (2, sibling))
+    ]
+    for copy in token_copies:
+        copy.start()
+    total[...] = jnp.zeros_like(total)
+    own_copy.wait()
+    for copy in token_copies:
+        copy.wait_recv()
+
+    def core_copy(j):
+        return remote(away.at[j], from_core.at[j], core_send.at[j], core_recv.at[j], batch=sibling)
+
+    def x_copy(j):
+        return remote(kept.at[j, block(1), :], from_x.at[j], x_send.at[j], x_recv.at[j], batch=across)
+
+    def hid_x(j):
+        return remote(hid.at[j, block(0), :], hid.at[j, block(1), :], hx_send.at[j], hx_recv.at[j], batch=across)
+
+    def hid_core(j):
+        return remote(hid.at[j, block(0), :], hid.at[j, block(2), :], hc_send.at[j], hc_recv.at[j], batch=sibling)
+
+    def hid_forward(j):
+        return remote(hid.at[j, block(1), :], hid.at[j, block(3), :], hf_send.at[j], hf_recv.at[j], batch=sibling)
+
+    def step(i, carry):
+        @pl.when(i < chunks)
+        def _():
+            for copy in gate_up(i):
+                copy.wait()
+            slot = lax.rem(i, SLOTS)
+            for part, ref in enumerate((gate_s, up_s)):
+                for n in range(width // tile):
+                    product = jnp.dot(
+                        acts[...], ref[slot, :, n * tile:(n + 1) * tile], preferred_element_type=f32
+                    ).astype(bf16)
+                    at = part * width + n * tile
+                    kept[i, :, at:at + tile] = product[:2 * rows]
+                    away[i, :, at:at + tile] = product[2 * rows:]
+            core_copy(i).start()
+
+            @pl.when(i + SLOTS < chunks)
+            def _():
+                for copy in gate_up(i + SLOTS):
+                    copy.start()
+
+        @pl.when((i >= 1) & (i < chunks + 1))
+        def _():
+            j = i - 1
+            core_copy(j).wait_recv()
+            kept[j, block(1), :] = (
+                kept[j, block(1), :].astype(f32) + from_core[j, block(1), :].astype(f32)
+            ).astype(bf16)
+            x_copy(j).start()
+
+        @pl.when((i >= LAG_C) & (i < chunks + LAG_C))
+        def _():
+            j = i - LAG_C
+            x_copy(j).wait_recv()
+            summed = (
+                kept[j, block(0), :].astype(f32) + from_core[j, block(0), :].astype(f32) + from_x[j].astype(f32)
+            )
+            gate, up = summed[:, :width], summed[:, width:]
+            hid[j, block(0), :] = (gate / (1.0 + jnp.exp(-gate)) * up).astype(bf16)
+            hid_x(j).start()
+            hid_core(j).start()
+
+        @pl.when((i >= LAG_D) & (i < chunks + LAG_D))
+        def _():
+            j = i - LAG_D
+            hid_x(j).wait_recv()
+            hid_forward(j).start()
+
+        @pl.when(i >= LAG_E)
+        def _():
+            j = i - LAG_E
+            slot = lax.rem(j, SLOTS)
+            down(j).wait()
+            hid_core(j).wait_recv()
+            hid_forward(j).wait_recv()
+            for n in range(depth // tile):
+                at = pl.ds(n * tile, tile)
+                total[:, at] += jnp.dot(hid[j], down_s[slot, :, at], preferred_element_type=f32)
+
+            @pl.when(j + SLOTS < chunks)
+            def _():
+                down(j + SLOTS).start()
+
+        return carry
+
+    lax.fori_loop(0, chunks + LAG_E, step, 0)
+
+    def place(m):
+        dx, dc = lax.rem(lax.div(m, 2) + x, 2), lax.rem(lax.rem(m, 2) + c, 2)
+        return pl.ds(pl.multiple_of((dc * 2 + dx) * rows, rows), rows)
+
+    def line_copy(way, m, to):
+        return remote(line_out.at[way, m], line_in.at[way, m], line_send.at[way, m], line_recv.at[way, m], mp=to)
+
+    def flow(way, m, sends, first, to):
+        @pl.when(sends)
+        def _():
+            line_out[way, m] = total[place(m), :].astype(bf16)
+
+            @pl.when(jnp.logical_not(first))
+            def _():
+                line_copy(way, m, to).wait_recv()
+                line_out[way, m] = (total[place(m), :] + line_in[way, m].astype(f32)).astype(bf16)
+
+            line_copy(way, m, to).start()
+
+    for k in range(mp - 1):
+        flow(0, mp - 1 - k, z < mp - 1 - k, z == 0, lax.rem(z + 1, mp))
+        flow(1, k, z > k, z == mp - 1, lax.rem(z + mp - 1, mp))
+
+    total[place(z), :] = total[place(z), :] + acts[place(z), :].astype(f32)
+
+    @pl.when(z > 0)
+    def _():
+        line_copy(0, z, lax.rem(z + 1, mp)).wait_recv()
+        total[place(z), :] = total[place(z), :] + line_in[0, z].astype(f32)
+
+    @pl.when(z < mp - 1)
+    def _():
+        line_copy(1, z, lax.rem(z + 1, mp)).wait_recv()
+        total[place(z), :] = total[place(z), :] + line_in[1, z].astype(f32)
+
+    out[...] = total[place(z), :].astype(bf16)
+
+    for copy in token_copies:
+        copy.wait_send()
+
+    def drain(j, carry):
+        for copy in (core_copy, x_copy, hid_x, hid_core, hid_forward):
+            copy(j).wait_send()
+        return carry
+
+    lax.fori_loop(0, chunks, drain, 0)
+    for k in range(mp - 1):
+        @pl.when(z < mp - 1 - k)
+        def _():
+            line_copy(0, mp - 1 - k, lax.rem(z + 1, mp)).wait_send()
+
+        @pl.when(z > k)
+        def _():
+            line_copy(1, k, lax.rem(z + mp - 1, mp)).wait_send()
+
+
+def fused(mp, chunks, tokens, gate_weight, up_weight, down_weight):
+    rows = tokens.shape[0]
+    depth, hidden = gate_weight.shape
+    width = hidden // chunks
+    bf16, dma = jnp.bfloat16, pltpu.SemaphoreType.DMA
+    return pl.pallas_call(
+        functools.partial(kernel, mp, chunks),
+        out_shape=jax.ShapeDtypeStruct((rows, depth), bf16),
+        in_specs=[pl.BlockSpec(memory_space=pl.ANY)] * 4,
+        out_specs=pl.BlockSpec(memory_space=pltpu.VMEM),
+        scratch_shapes=[
+            pltpu.VMEM((4 * rows, depth), bf16),
+            pltpu.VMEM((SLOTS, depth, width), bf16),
+            pltpu.VMEM((SLOTS, depth, width), bf16),
+            pltpu.VMEM((SLOTS, width, depth), bf16),
+            pltpu.VMEM((chunks, 2 * rows, 2 * width), bf16),
+            pltpu.VMEM((chunks, 2 * rows, 2 * width), bf16),
+            pltpu.VMEM((chunks, 2 * rows, 2 * width), bf16),
+            pltpu.VMEM((chunks, rows, 2 * width), bf16),
+            pltpu.VMEM((chunks, 4 * rows, width), bf16),
+            pltpu.VMEM((4 * rows, depth), jnp.float32),
+            pltpu.VMEM((2, mp, rows, depth), bf16),
+            pltpu.VMEM((2, mp, rows, depth), bf16),
+            dma(()),
+            dma((SLOTS,)), dma((SLOTS,)), dma((SLOTS,)),
+            dma((4,)), dma((4,)),
+        ] + [dma((chunks,))] * 10 + [dma((2, mp)), dma((2, mp))],
+        compiler_params=pltpu.CompilerParams(
+            collective_id=0, has_side_effects=True, vmem_limit_bytes=56 * 2**20
+        ),
+        cost_estimate=pl.CostEstimate(
+            flops=4 * rows * depth * hidden * 6, bytes_accessed=6 * depth * hidden, transcendentals=rows * hidden
+        ),
+    )(tokens, gate_weight, up_weight, down_weight)
+
+
+def plain(tokens, gate_weight, up_weight, down_weight):
     hidden_width = gate_weight.shape[1]
     exchanged = lax.all_to_all(tokens, "batch", split_axis=1, concat_axis=0, tiled=True)
     both_weights = jnp.concatenate([gate_weight, up_weight], axis=1)
@@ -30,6 +289,8 @@
 
 def solution(mesh):
     placed = (P(("groups", "batch"), None), P("batch", "mp"), P("batch", "mp"), P("mp", "batch"))
+    batch, mp = mesh.shape["batch"], mesh.shape["mp"]
+    local = functools.partial(fused, mp, 13) if batch == 4 and mp == 4 else plain
     return jax.shard_map(
         local, mesh=mesh, in_specs=placed, out_specs=P(("groups", "mp"), "batch"), check_vma=False
     )

time: 211 us -> 112 us (0.53)
  waiting for transfers between devices: 120 us -> 0 us
  Pallas kernels: 0 us -> 110 us
  matrix products: 43.1 us -> 0 us
  blocking collectives: 18.5 us -> 0 us
  between operations: 13.1 us -> 0.01 us
  local copies, waits for them, and re-layouts: 11.3 us -> 1.67 us
  other arithmetic: 4.76 us -> 0 us
    pallas_call x0 -> x1, Pallas kernels: none -> 110 us  [fused(): pl.pallas_call(functools.partial(kernel, mp, chunks), out_shape=jax.Shape...]
    reduce_scatter x2 -> x0, waiting for transfers between devices: 89.6 us -> none  [the longest x1 62.3 us: local(): lax.psum_scatter(jnp.dot(exchanged, both_weights, preferred_element_type=...]
    dot_general x2 -> x0, matrix products: 43.1 us -> none  [the longest x1 28.8 us: local(): jnp.dot(exchanged, both_weights, preferred_element_type=jnp.float32)]
    all_gather x1 -> x0, waiting for transfers between devices: 30.1 us -> none  [local(): lax.all_gather(hidden, 'batch', axis=0, tiled=True)]
    all_to_all x1 -> x0, blocking collectives: 18.5 us -> none  [local(): lax.all_to_all(tokens, 'batch', split_axis=1, concat_axis=0, tiled=True)]
    unnamed x1, local copies, waits for them, and re-layouts: 9.97 us -> 1.67 us
    convert_element_type x3 -> x0, other arithmetic: 4.76 us -> none  [the longest x1 1.71 us: local(): return (own_part.astype(jnp.float32) + shared).astype(jnp.bfloat16)]
  transfers between devices with their start and end apart: 3 -> 0, of which waited for: 3 -> 0; matrix products, arithmetic and copies ran while one was open for 0% -> 0% of each run, Pallas kernels for 0% -> 0%
where the time goes in v1:
time: 112 us
  Pallas kernels  110 us (98%)
  local copies, waits for them, and re-layouts  1.67 us (1%)
    pallas_call x1, Pallas kernels, fused(): pl.pallas_call(functools.partial(kernel, mp, chunks), out_shape=jax.Shape...  110 us

profile of v1, /device:TPU:0, one launch (start us, length us, event | category | flops | bytes accessed | tf_op | source)
XLA Modules:
  0.0 112.2 jit_solution(5582738520661171510)
XLA Ops:
  0.0 110.5 %shard_map.46 = bf16[64,2048]{1,0:T(8,128)(2,1)} custom-call(bf16[64,8192]{1,0:T(8,128)(2,1)} %tokens.1, bf16[2048,6656]{1,0:T(8,128)(2,1)} %gate_w.1, bf16[2048,6656]{1,0:T(8,128)(2,1)} %up_w.1, bf16[6656,2048]{1,0:T(8,128)(2,1)} %down_w.1), custom_call_target="tpu_custom_call" | custom-call | flops 20937965568 | bytes 81788928 | tf_op jit(solution)/shard_map/pallas_call | solution.py:235
  110.5 1.7 %copy.6 = bf16[64,2048]{1,0:T(8,128)(2,1)} copy(bf16[64,2048]{1,0:T(8,128)(2,1)} %shard_map.46) | data formatting | bytes 524288

commit v2 on v1

--- a/solution.py
+++ b/solution.py
@@ -9,15 +9,15 @@
 
 MESH = pl.DeviceIdType.MESH
 SLOTS = 3
-LAG_C, LAG_D, LAG_E = 3, 4, 5
+LAG_C, LAG_D, LAG_E = 2, 3, 4
 
 
 def kernel(
     mp, chunks, tokens, gate_w, up_w, down_w, out,
-    acts, gate_s, up_s, down_s, away, kept, from_core, from_x, hid, total, line_out, line_in,
+    acts, gate_s, up_s, down_s, away, kept, from_core, from_x, hid, total, term_out, term_in,
     own_sem, gate_sem, up_sem, down_sem, tok_send, tok_recv,
     core_send, core_recv, x_send, x_recv, hx_send, hx_recv, hc_send, hc_recv, hf_send, hf_recv,
-    line_send, line_recv,
+    term_send, term_recv,
 ):
     f32, bf16 = jnp.float32, jnp.bfloat16
     me, z = lax.axis_index("batch"), lax.axis_index("mp")
@@ -62,21 +62,9 @@
     for peer in (sibling, across, diagonal):
         pl.semaphore_signal(barrier, inc=1, device_id={"batch": peer}, device_id_type=MESH)
 
-    @pl.when(z > 0)
-    def _():
-        pl.semaphore_signal(barrier, inc=1, device_id={"mp": z - 1}, device_id_type=MESH)
-
-    @pl.when(z < mp - 1)
-    def _():
-        pl.semaphore_signal(barrier, inc=1, device_id={"mp": z + 1}, device_id_type=MESH)
-
-    @pl.when((z > 0) & (z < mp - 1))
-    def _():
-        pl.semaphore_wait(barrier, 5)
-
-    @pl.when((z == 0) | (z == mp - 1))
-    def _():
-        pl.semaphore_wait(barrier, 4)
+    for d in range(1, mp):
+        pl.semaphore_signal(barrier, inc=1, device_id={"mp": lax.rem(z + d, mp)}, device_id_type=MESH)
+    pl.semaphore_wait(barrier, 3 + mp - 1)
 
     token_copies = [
         remote(tokens.at[:, columns(peer)], acts.at[block(r), :], tok_send.at[r], tok_recv.at[r], batch=peer)
@@ -175,38 +163,19 @@
         dx, dc = lax.rem(lax.div(m, 2) + x, 2), lax.rem(lax.rem(m, 2) + c, 2)
         return pl.ds(pl.multiple_of((dc * 2 + dx) * rows, rows), rows)
 
-    def line_copy(way, m, to):
-        return remote(line_out.at[way, m], line_in.at[way, m], line_send.at[way, m], line_recv.at[way, m], mp=to)
-
-    def flow(way, m, sends, first, to):
-        @pl.when(sends)
-        def _():
-            line_out[way, m] = total[place(m), :].astype(bf16)
-
-            @pl.when(jnp.logical_not(first))
-            def _():
-                line_copy(way, m, to).wait_recv()
-                line_out[way, m] = (total[place(m), :] + line_in[way, m].astype(f32)).astype(bf16)
-
-            line_copy(way, m, to).start()
-
-    for k in range(mp - 1):
-        flow(0, mp - 1 - k, z < mp - 1 - k, z == 0, lax.rem(z + 1, mp))
-        flow(1, k, z > k, z == mp - 1, lax.rem(z + mp - 1, mp))
-
-    total[place(z), :] = total[place(z), :] + acts[place(z), :].astype(f32)
-
-    @pl.when(z > 0)
-    def _():
-        line_copy(0, z, lax.rem(z + 1, mp)).wait_recv()
-        total[place(z), :] = total[place(z), :] + line_in[0, z].astype(f32)
-
-    @pl.when(z < mp - 1)
-    def _():
-        line_copy(1, z, lax.rem(z + 1, mp)).wait_recv()
-        total[place(z), :] = total[place(z), :] + line_in[1, z].astype(f32)
-
-    out[...] = total[place(z), :].astype(bf16)
+    def term_copy(d):
+        return remote(
+            term_out.at[d - 1], term_in.at[d - 1], term_send.at[d - 1], term_recv.at[d - 1], mp=lax.rem(z + d, mp)
+        )
+
+    for d in range(1, mp):
+        term_out[d - 1] = total[place(lax.rem(z + d, mp)), :].astype(bf16)
+        term_copy(d).start()
+    mine = total[place(z), :] + acts[place(z), :].astype(f32)
+    for d in range(1, mp):
+        term_copy(d).wait_recv()
+        mine = mine + term_in[d - 1].astype(f32)
+    out[...] = mine.astype(bf16)
 
     for copy in token_copies:
         copy.wait_send()
@@ -217,14 +186,8 @@
         return carry
 
     lax.fori_loop(0, chunks, drain, 0)
-    for k in range(mp - 1):
-        @pl.when(z < mp - 1 - k)
-        def _():
-            line_copy(0, mp - 1 - k, lax.rem(z + 1, mp)).wait_send()
-
-        @pl.when(z > k)
-        def _():
-            line_copy(1, k, lax.rem(z + mp - 1, mp)).wait_send()
+    for d in range(1, mp):
+        term_copy(d).wait_send()
 
 
 def fused(mp, chunks, tokens, gate_weight, up_weight, down_weight):
@@ -248,12 +211,12 @@
             pltpu.VMEM((chunks, rows, 2 * width), bf16),
             pltpu.VMEM((chunks, 4 * rows, width), bf16),
             pltpu.VMEM((4 * rows, depth), jnp.float32),
-            pltpu.VMEM((2, mp, rows, depth), bf16),
-            pltpu.VMEM((2, mp, rows, depth), bf16),
+            pltpu.VMEM((mp - 1, rows, depth), bf16),
+            pltpu.VMEM((mp - 1, rows, depth), bf16),
             dma(()),
             dma((SLOTS,)), dma((SLOTS,)), dma((SLOTS,)),
             dma((4,)), dma((4,)),
-        ] + [dma((chunks,))] * 10 + [dma((2, mp)), dma((2, mp))],
+        ] + [dma((chunks,))] * 10 + [dma((mp - 1,)), dma((mp - 1,))],
         compiler_params=pltpu.CompilerParams(
             collective_id=0, has_side_effects=True, vmem_limit_bytes=56 * 2**20
         ),

time: 112 us -> 107 us (0.955)
  the two profiles are of different devices: /device:TPU:0 before, /device:TPU:9 now
where the time goes in v2:
time: 107 us; the launch traced here: 106 us
  Pallas kernels  105 us (98%)
  local copies, waits for them, and re-layouts  1.67 us (2%)
    pallas_call x1, Pallas kernels, fused(): pl.pallas_call(functools.partial(kernel, mp, chunks), out_shape=jax.Shape...  105 us

profile of v2, /device:TPU:9, one launch (start us, length us, event | category | flops | bytes accessed | tf_op | source)
XLA Modules:
  0.0 106.4 jit_solution(4489389024597306243)
XLA Ops:
  0.0 104.7 %shard_map.46 = bf16[64,2048]{1,0:T(8,128)(2,1)} custom-call(bf16[64,8192]{1,0:T(8,128)(2,1)} %tokens.1, bf16[2048,6656]{1,0:T(8,128)(2,1)} %gate_w.1, bf16[2048,6656]{1,0:T(8,128)(2,1)} %up_w.1, bf16[6656,2048]{1,0:T(8,128)(2,1)} %down_w.1), custom_call_target="tpu_custom_call" | custom-call | flops 20937965568 | bytes 81788928 | tf_op jit(solution)/shard_map/pallas_call | solution.py:198
  104.7 1.7 %copy.6 = bf16[64,2048]{1,0:T(8,128)(2,1)} copy(bf16[64,2048]{1,0:T(8,128)(2,1)} %shard_map.46) | data formatting | bytes 524288
